TPU v7x, 32 devices: a whole 2x2x4 slice. The times are simulated.
32 devices in a mesh: dp: 4 (over y, x), ctx: 8 (over z, core).
Axes of the slice: x: 2, y: 2, z: 4, core: 2. Of those that a mesh axis runs over, the one named last changes fastest.
Arguments:
- retained_indices: int32 [4, 768], P('dp'), may hold values from 0 to 1535, as said below
- projected_result_derivative: bfloat16 [4, 1536, 2560], P('dp', 'ctx'), may hold values from -6 to 6
- head_to_model_projector: bfloat16 [4096, 2560], P('ctx'), may hold values from -0.09375 to 0.09375
- retained_queries_saved: bfloat16 [4, 768, 4096], P('dp', None, 'ctx'), may hold values from -54 to 54
- retained_keys_saved: bfloat16 [4, 768, 4096], P('dp', None, 'ctx'), may hold values from -6 to 6
- retained_values_saved: bfloat16 [4, 768, 4096], P('dp', None, 'ctx'), may hold values from -6 to 6
Outputs:
- derivative_every_place: bfloat16 [4, 1536, 12288], P('dp', 'ctx')
- projector_derivative: float32 [4096, 2560], P('ctx')
Inputs may be any that keep to these rules, and one draw needn't show every extreme that they name: `retained_indices`: each row lists 768 distinct positions in increasing order. The 192 positions of one device, an aligned block, hold from 48 to 144 of them, and in every sequence some device holds exactly 144.
All inputs are finite; a program needn't handle non-finite values.
Results may differ from a plain program's by a relative error of at most 0.017.
Values may be sent and summed in bfloat16 or wider, within the bound.
A program may use at most 128 MiB of HBM per device.

v0:
```python
import math

import jax
import jax.numpy as jnp
from jax import lax
from jax.sharding import PartitionSpec as P

HEAD_DIM = 128


def make_projector(head_to_model_projector):

    def project(portion, offset):
        products = jnp.einsum(
            "rw,hw->rh", portion, head_to_model_projector, preferred_element_type=jnp.float32
        )
        return jnp.concatenate([portion, products.astype(jnp.bfloat16)], axis=1)

    return project


def heads_backward(query_rows, key_rows, value_rows, head_grads):
    surv_count, local_width = query_rows.shape
    heads_here = local_width // HEAD_DIM
    scale_factor = 1.0 / math.sqrt(HEAD_DIM)
    block_rows = 512 if surv_count % 512 == 0 else surv_count
    keys_three = key_rows.reshape(surv_count, heads_here, HEAD_DIM)
    values_three = value_rows.reshape(surv_count, heads_here, HEAD_DIM)
    key_index = jnp.arange(surv_count, dtype=jnp.int32)

    def one_block(carry, block_id):
        grad_keys, grad_values = carry
        offset = block_id * block_rows
        query_block = lax.dynamic_slice_in_dim(query_rows, offset, block_rows, 0).reshape(
            block_rows, heads_here, HEAD_DIM
        )
        grad_block = lax.dynamic_slice_in_dim(head_grads, offset, block_rows, 0).reshape(
            block_rows, heads_here, HEAD_DIM
        )
        scores = (
            jnp.einsum("qhd,khd->hqk", query_block, keys_three, preferred_element_type=jnp.float32)
            * scale_factor
        )
        query_index = offset + jnp.arange(block_rows, dtype=jnp.int32)
        allowed = key_index[None, :] <= query_index[:, None]
        scores = jnp.where(allowed[None], scores, -jnp.inf)
        row_max = jnp.max(scores, axis=-1, keepdims=True)
        exponent = jnp.exp(scores - row_max)
        probs = exponent / jnp.sum(exponent, axis=-1, keepdims=True)
        probs_low = probs.astype(jnp.bfloat16)
        output = jnp.einsum(
            "hqk,khd->qhd", probs_low, values_three, preferred_element_type=jnp.float32
        ).astype(jnp.bfloat16)
        dprobs = jnp.einsum(
            "qhd,khd->hqk", grad_block, values_three, preferred_element_type=jnp.float32
        )
        center = jnp.sum(probs * dprobs, axis=-1, keepdims=True)
        dscores = (probs * (dprobs - center) * scale_factor).astype(jnp.bfloat16)
        grad_query = jnp.einsum(
            "hqk,khd->qhd", dscores, keys_three, preferred_element_type=jnp.float32
        ).astype(jnp.bfloat16)
        grad_keys = grad_keys + jnp.einsum(
            "hqk,qhd->khd", dscores, query_block, preferred_element_type=jnp.float32
        )
        grad_values = grad_values + jnp.einsum(
            "hqk,qhd->khd", probs_low, grad_block, preferred_element_type=jnp.float32
        )
        return (
            (grad_keys, grad_values),
            (output.reshape(block_rows, local_width), grad_query.reshape(block_rows, local_width)),
        )

    zero_state = jnp.zeros((surv_count, heads_here, HEAD_DIM), jnp.float32)
    final_state, block_results = lax.scan(
        one_block, (zero_state, zero_state), jnp.arange(surv_count // block_rows, dtype=jnp.int32)
    )
    outputs = block_results[0].reshape(surv_count, local_width)
    grad_query = block_results[1].reshape(surv_count, local_width)
    grad_key = final_state[0].reshape(surv_count, local_width).astype(jnp.bfloat16)
    grad_value = final_state[1].reshape(surv_count, local_width).astype(jnp.bfloat16)
    return (outputs, grad_query, grad_key, grad_value)


def body(
    retained_indices,
    projected_result_derivative,
    head_to_model_projector,
    retained_queries_saved,
    retained_keys_saved,
    retained_values_saved,
):
    shard_count = lax.axis_size("ctx")
    sequence_places = retained_indices[0]
    surv_count = sequence_places.shape[0]
    rows_here = projected_result_derivative.shape[1]
    width_model = projected_result_derivative.shape[2]
    local_width = retained_queries_saved.shape[2]
    shard_ids = jnp.arange(shard_count, dtype=jnp.int32)
    project = make_projector(head_to_model_projector)
    combined = project(
        lax.all_gather(projected_result_derivative[0], "ctx", axis=0, tiled=True), jnp.int32(0)
    )
    picked_rows = combined[sequence_places]
    picked = picked_rows[:, :width_model]
    head_grads = picked_rows[:, width_model:]
    outputs, grad_query, grad_key, grad_value = heads_backward(
        retained_queries_saved[0], retained_keys_saved[0], retained_values_saved[0], head_grads
    )
    partial_grad = jnp.einsum("sh,sw->hw", outputs, picked, preferred_element_type=jnp.float32)
    projector_derivative = lax.psum(partial_grad.astype(jnp.bfloat16), "dp").astype(jnp.float32)
    inverse = (
        jnp.full((shard_count * rows_here,), -1, jnp.int32)
        .at[sequence_places]
        .set(jnp.arange(surv_count, dtype=jnp.int32))
    )
    position_grid = jnp.arange(rows_here, dtype=jnp.int32)[:, None] + shard_ids[None, :] * rows_here
    found_index = inverse[position_grid]
    valid_rows = found_index >= 0
    safe_found = jnp.clip(found_index, 0, surv_count - 1)

    def pack_all(matrix):
        return jnp.where(valid_rows[:, :, None], matrix[safe_found], jnp.zeros((), jnp.bfloat16))

    received = (
        lax.all_to_all(pack_all(grad_query), "ctx", split_axis=1, concat_axis=1, tiled=True),
        lax.all_to_all(pack_all(grad_key), "ctx", split_axis=1, concat_axis=1, tiled=True),
        lax.all_to_all(pack_all(grad_value), "ctx", split_axis=1, concat_axis=1, tiled=True),
    )
    derivative_every_place = jnp.concatenate(
        [part_grad.reshape(rows_here, shard_count * local_width) for part_grad in received], axis=1
    )
    return (derivative_every_place[None], projector_derivative)


def solution(mesh):
    in_specs = (
        P("dp", None),
        P("dp", "ctx", None),
        P("ctx", None),
        P("dp", None, "ctx"),
        P("dp", None, "ctx"),
        P("dp", None, "ctx"),
    )
    out_specs = (P("dp", "ctx", None), P("ctx", None))
    return jax.shard_map(body, mesh=mesh, in_specs=in_specs, out_specs=out_specs, check_vma=False)
```

profile of v0, /device:TPU:11, one launch (start us, length us, event | category | flops | bytes accessed | tf_op | source)
XLA Modules:
  0.0 384.6 jit_solution(6419557177570801716)
XLA Ops:
  7.9 1.5 copy.89
  9.4 2.3 copy.87
  11.7 2.3 copy.88
  14.1 3.4 scatter_custom_fusion
  17.6 8.4 %gather_fusion = s32[1536]{0:T(1024)S(1)} fusion(s32[1536]{0:T(1024)S(1)} %scatter_custom_fusion, s32[2048]{0:T(1024)S(1)} %pad_clamp_fusion.1), kind=kCustom, calls=%fused_computation | custom fusion | bytes 18432 | tf_op jit(solution)/shard_map/gather | solution.py:117
  28.9 8.4 %fusion.44 = (f32[4,768]{1,0:T(4,128)S(1)}, f32[4,768,768]{1,2,0:T(8,128)}) fusion(pred[768,768]{0,1:T(8,128)(4,1)} %iota_compare_fusion, bf16[768,4,128]{0,2,1:T(8,128)(2,1)} %bitcast.62, bf16[768,4,128]{0,2,1:T(8,128)(2,1)} %bitcast.60), kind=kOutput, calls=%fused_computation.57 | convolution fusion | flops 613417728 | bytes 11612160 | tf_op jit(solution)/shard_map/while/body/eval_jaxpr/sub | solution.py:48
  37.3 49.3 %all-gather.3.cloned.1.call-done = bf16[1,1536,2560]{2,1,0:T(8,128)(2,1)} async-done(((bf16[1,192,2560]{2,1,0:T(8,128)(2,1)}), bf16[1,1536,2560]{2,1,0:T(8,128)(2,1)}) %all-gather.3.cloned.1.call-update) | async-done | bytes 7864336 | tf_op jit(solution)/shard_map/all_gather | solution.py:101
  86.6 8.6 %convolution_convert_fusion.1 = bf16[1536,512]{0,1:T(8,128)(2,1)} fusion(bf16[512,2560]{1,0:T(8,128)(2,1)S(1)} %copy-done, bf16[1,1536,2560]{2,1,0:T(8,128)(2,1)} %all-gather.3.cloned.1.call-done), kind=kOutput, calls=%fused_computation.25 | convolution fusion | flops 4027318272 | bytes 12058624 | tf_op jit(solution)/shard_map/rw,hw->rh/dot_general | solution.py:14
  95.2 1.7 copy.62
  96.9 8.7 %pad_maximum_fusion = bf16[1536,3072]{1,0:T(8,128)(2,1)} fusion(bf16[1536,512]{1,0:T(8,128)(2,1)S(1)} %copy.62, bf16[1536,2560]{1,0:T(8,128)(2,1)} %bitcast.48), kind=kLoop, calls=%fused_computation.8 | loop fusion | flops 18874368 | bytes 18874368 | tf_op jit(solution)/shard_map/concatenate | solution.py:17
  105.6 14.6 %gather_fusion.1 = bf16[768,3072]{1,0:T(8,128)(2,1)} fusion(bf16[1536,3072]{1,0:T(8,128)(2,1)} %pad_maximum_fusion, s32[1024]{0:T(1024)S(1)} %pad_clamp_fusion.2), kind=kCustom, calls=%fused_computation.1 | custom fusion | bytes 9440256 | tf_op jit(solution)/shard_map/gather | solution.py:103
  121.7 5.1 %fusion.45 = f32[4,768,768]{1,2,0:T(8,128)} fusion(bf16[768,4,128]{0,2,1:T(8,128)(2,1)S(1)} %bitcast.56, bf16[768,4,128]{0,2,1:T(8,128)(2,1)S(1)} %bitcast.58), kind=kOutput, calls=%fused_computation.58 | convolution fusion | flops 603979776 | bytes 11010048 | tf_op jit(solution)/shard_map/while/body/eval_jaxpr/qhd,khd->hqk/dot_general | solution.py:54
  126.8 14.6 %fusion.31 = bf16[4,768,128]{1,2,0:T(8,128)(2,1)} fusion(bf16[768,4,128]{0,2,1:T(8,128)(2,1)S(1)} %bitcast.63, f32[4,768,768]{1,2,0:T(8,128)} %fusion.45, f32[4,768,768]{1,2,0:T(8,128)} %get-tuple-element.26, f32[4,768]{1,0:T(4,128)S(1)} %get-tuple-element.25), kind=kOutput, calls=%fused_computation.37 | convolution fusion | flops 620891904 | bytes 20459520 | tf_op jit(solution)/shard_map/while/body/eval_jaxpr/hqk,qhd->khd/dot_general | solution.py:62
  141.4 15.9 %fusion.28 = bf16[4,768,128]{1,2,0:T(8,128)(2,1)} fusion(bf16[768,4,128]{0,2,1:T(8,128)(2,1)S(1)} %bitcast.61, f32[4,768,768]{1,2,0:T(8,128)} %fusion.45, f32[4,768,768]{1,2,0:T(8,128)} %get-tuple-element.26, f32[4,768]{1,0:T(4,128)S(1)} %get-tuple-element.25), kind=kOutput, calls=%fused_computation.36 | convolution fusion | flops 620891904 | bytes 20459520 | tf_op jit(solution)/shard_map/while/body/eval_jaxpr/hqk,khd->qhd/dot_general | solution.py:59
  157.4 5.3 %fusion.22 = bf16[4,128,768]{2,1,0:T(8,128)(2,1)S(1)} fusion(bf16[768,4,128]{0,2,1:T(8,128)(2,1)S(1)} %bitcast.59, f32[4,768,768]{1,2,0:T(8,128)} %get-tuple-element.26, f32[4,768]{1,0:T(4,128)S(1)} %get-tuple-element.25), kind=kOutput, calls=%fused_computation.34 | convolution fusion | flops 609091584 | bytes 11022336 | tf_op jit(solution)/shard_map/while/body/eval_jaxpr/hqk,qhd->khd/dot_general | solution.py:65
  162.7 1.4 copy.73
  164.1 1.4 copy.68
  165.6 5.4 %gather_fusion.3 = bf16[1536,512]{1,0:T(8,128)(2,1)} fusion(bf16[768,512]{1,0:T(8,128)(2,1)S(1)} %copy.73, s32[2048]{0:T(1024)S(1)} %pad_clamp_fusion), kind=kCustom, calls=%fused_computation.3 | custom fusion | bytes 3151872 | tf_op jit(solution)/shard_map/gather | solution.py:122
  171.0 5.4 %gather_fusion.2 = bf16[1536,512]{1,0:T(8,128)(2,1)} fusion(bf16[768,512]{1,0:T(8,128)(2,1)S(1)} %copy.68, s32[2048]{0:T(1024)S(1)} %pad_clamp_fusion), kind=kCustom, calls=%fused_computation.2 | custom fusion | bytes 3151872 | tf_op jit(solution)/shard_map/gather | solution.py:122
  176.7 5.4 %gather_fusion.4 = bf16[1536,512]{1,0:T(8,128)(2,1)} fusion(bf16[768,512]{1,0:T(8,128)(2,1)S(1)} %copy.77, s32[2048]{0:T(1024)S(1)} %pad_clamp_fusion), kind=kCustom, calls=%fused_computation.4 | custom fusion | bytes 3151872 | tf_op jit(solution)/shard_map/gather | solution.py:122
  182.1 6.8 %copy_select_fusion.2 = (bf16[192,8,512]{2,0,1:T(8,128)(2,1)S(1)}, bf16[192,8,512]{2,0,1:T(8,128)(2,1)}, bf16[192,8,512]{2,0,1:T(8,128)(2,1)}) fusion(bf16[192,8,512]{2,1,0:T(8,128)(2,1)} %bitcast.50, pred[192,8]{0,1:T(8,128)(4,1)S(1)} %copy.59, bf16[192,8,512]{2,1,0:T(8,128)(2,1)S(1)} %bitcast.49, bf16[192,8,512]{2,1,0:T(8,128)(2,1)} %bitcast.51), kind=kLoop, calls=%fused_computation.33 | loop fusion | flops 2359296 | bytes 9438720 | tf_op jit(solution)/shard_map/jit(_where)/select_n | solution.py:122
  188.9 40.0 %all_to_all.15 = bf16[192,8,512]{2,0,1:T(8,128)(2,1)S(1)} all-to-all(bf16[192,8,512]{2,0,1:T(8,128)(2,1)S(1)} %get-tuple-element.22), channel_id=1, replica_groups=mesh['dp'=4,'ctx'=8] {'ctx'}, dimensions={1} | all-to-all | bytes 3145728 | tf_op jit(solution)/shard_map/all_to_all | solution.py:125
  228.9 7.3 %all-to-all-start.1 = ((bf16[192,8,512]{2,0,1:T(8,128)(2,1)}), bf16[192,8,512]{2,0,1:T(8,128)(2,1)}, u32[]{:S(2)}, u32[]{:S(2)}) async-start(bf16[192,8,512]{2,0,1:T(8,128)(2,1)} %get-tuple-element.23), calls=%async_computation.1 | async-start | bytes 3145728 | tf_op jit(solution)/shard_map/all_to_all | solution.py:126
  236.2 4.6 %fusion.25 = bf16[4,768,128]{1,2,0:T(8,128)(2,1)S(1)} fusion(bf16[768,4,128]{0,2,1:T(8,128)(2,1)S(1)} %bitcast.57, f32[4,768,768]{1,2,0:T(8,128)} %get-tuple-element.26, f32[4,768]{1,0:T(4,128)S(1)} %get-tuple-element.25), kind=kOutput, calls=%fused_computation.35 | convolution fusion | flops 609091584 | bytes 11022336 | tf_op jit(solution)/shard_map/while/body/eval_jaxpr/hqk,khd->qhd/dot_general | solution.py:51
  240.8 29.7 %all-to-all-done.1 = bf16[192,8,512]{2,0,1:T(8,128)(2,1)} async-done(((bf16[192,8,512]{2,0,1:T(8,128)(2,1)}), bf16[192,8,512]{2,0,1:T(8,128)(2,1)}, u32[]{:S(2)}, u32[]{:S(2)}) %all-to-all-start.1) | async-done | bytes 1572896 | tf_op jit(solution)/shard_map/all_to_all | solution.py:126
  270.5 7.9 %all-to-all-start.2 = ((bf16[192,8,512]{2,0,1:T(8,128)(2,1)}), bf16[192,8,512]{2,0,1:T(8,128)(2,1)}, u32[]{:S(2)}, u32[]{:S(2)}) async-start(bf16[192,8,512]{2,0,1:T(8,128)(2,1)} %get-tuple-element.24), calls=%async_computation.2 | async-start | bytes 3145728 | tf_op jit(solution)/shard_map/all_to_all | solution.py:127
  278.3 5.8 %convolution_convert_fusion = bf16[512,2560]{1,0:T(8,128)(2,1)} fusion(bf16[768,512]{0,1:T(8,128)(2,1)S(1)} %bitcast.67, bf16[768,3072]{1,0:T(8,128)(2,1)} %gather_fusion.1), kind=kOutput, calls=%fused_computation.20 | convolution fusion | flops 2014576640 | bytes 7340032 | tf_op jit(solution)/shard_map/sh,sw->hw/dot_general | solution.py:109
  284.2 79.2 %all-reduce.2.cloned.1.call-done = bf16[512,2560]{1,0:T(8,128)(2,1)} async-done(((bf16[512,2560]{1,0:T(8,128)(2,1)}), bf16[512,2560]{1,0:T(8,128)(2,1)}) %all-reduce.2.cloned.1.call-update) | async-done | bytes 2621456 | tf_op jit(solution)/shard_map/psum | solution.py:110
  363.3 4.8 %convert_element_type.63 = f32[512,2560]{1,0:T(8,128)} convert(bf16[512,2560]{1,0:T(8,128)(2,1)} %all-reduce.2.cloned.1.call-done) | non-fusion elementwise | flops 1310720 | bytes 7864320 | tf_op jit(solution)/shard_map/convert_element_type | solution.py:110
  369.5 2.8 copy.91
  372.3 1.7 copy.92
  374.0 3.8 maximum_bitcast_fusion
  (37 shorter events, 7.0 us)
Async XLA Ops:
  7.2 79.4 %copy-start = (bf16[512,2560]{1,0:T(8,128)(2,1)S(1)}, bf16[512,2560]{1,0:T(8,128)(2,1)}, u32[]{:S(2)}) copy-start(bf16[512,2560]{1,0:T(8,128)(2,1)} %param.8) | copy-start | bytes 7864324
  7.2 6.9 %copy-start.5 = (s32[1,768]{1,0:T(1,128)S(1)}, s32[1,768]{1,0:T(1,128)}, u32[]{:S(2)}) copy-start(s32[1,768]{1,0:T(1,128)} %param.6) | copy-start | bytes 9220
  7.2 79.4 %all-gather.3.cloned.1.call-start = ((), (), s32[]{:S(2)}) async-start(), calls=%async_computation.4 | async-start | bytes 8847360 | tf_op jit(solution)/shard_map/all_gather | solution.py:101
  121.7 5.1 %copy-start.4 = (bf16[1,768,512]{1,2,0:T(8,128)(2,1)S(1)}, bf16[1,768,512]{1,2,0:T(8,128)(2,1)}, u32[]{:S(2)}) copy-start(bf16[1,768,512]{1,2,0:T(8,128)(2,1)} %copy.88) | copy-start | bytes 2359300
  126.8 14.6 %copy-start.3 = (bf16[1,768,512]{1,2,0:T(8,128)(2,1)S(1)}, bf16[1,768,512]{1,2,0:T(8,128)(2,1)}, u32[]{:S(2)}) copy-start(bf16[1,768,512]{1,2,0:T(8,128)(2,1)} %copy.87) | copy-start | bytes 2359300
  176.7 5.4 %copy-start.2 = (bf16[1536,512]{1,0:T(8,128)(2,1)S(1)}, bf16[1536,512]{1,0:T(8,128)(2,1)}, u32[]{:S(2)}) copy-start(bf16[1536,512]{1,0:T(8,128)(2,1)} %gather_fusion.3) | copy-start | bytes 4718596
  228.9 41.6 %all-to-all-start.1 = ((bf16[192,8,512]{2,0,1:T(8,128)(2,1)}), bf16[192,8,512]{2,0,1:T(8,128)(2,1)}, u32[]{:S(2)}, u32[]{:S(2)}) async-start(bf16[192,8,512]{2,0,1:T(8,128)(2,1)} %get-tuple-element.23), calls=%async_computation.1 | async-start | bytes 3145728 | tf_op jit(solution)/shard_map/all_to_all | solution.py:126
  270.5 101.8 %all-to-all-start.2 = ((bf16[192,8,512]{2,0,1:T(8,128)(2,1)}), bf16[192,8,512]{2,0,1:T(8,128)(2,1)}, u32[]{:S(2)}, u32[]{:S(2)}) async-start(bf16[192,8,512]{2,0,1:T(8,128)(2,1)} %get-tuple-element.24), calls=%async_computation.2 | async-start | bytes 3145728 | tf_op jit(solution)/shard_map/all_to_all | solution.py:127
  278.3 85.0 %all-reduce.2.cloned.1.call-start = ((), (), s32[]{:S(2)}) async-start(), calls=%async_computation.3 | async-start | bytes 5242880 | tf_op jit(solution)/shard_map/psum | solution.py:110
  372.3 5.5 %copy-start.1 = (bf16[512,2560]{1,0:T(8,128)(2,1)S(1)}, bf16[512,2560]{1,0:T(8,128)(2,1)}, u32[]{:S(2)}) copy-start(bf16[512,2560]{1,0:T(8,128)(2,1)} %param.8) | copy-start | bytes 7864324
Sparse Core Ops, SparseCore 0:
  9.7 76.8 all-gather.2
  284.3 79.0 all-reduce.1
where the time goes:
time: 387 us; the launch traced here: 385 us
  waiting for transfers between devices  159 us (41%)
  matrix products  68.4 us (18%)
  local copies, waits for them, and re-layouts  62.2 us (16%)
  blocking collectives  40 us (10%)
  other arithmetic  25.8 us (7%)
  starting transfers between devices  15.2 us (4%)
  between operations  14.2 us (4%)
    psum x1, waiting for transfers between devices, body(): lax.psum(partial_grad.astype(jnp.bfloat16), 'dp').astype(jnp.float32)  79.2 us
    all_gather x1, waiting for transfers between devices, body(): lax.all_gather(projected_result_derivative[0], 'ctx', axis=0, tiled=True)  49.3 us
    all_to_all x1, blocking collectives, body(): lax.all_to_all(pack_all(grad_query), 'ctx', split_axis=1, concat_axis=1,...  40 us
    all_to_all x1, waiting for transfers between devices, body(): lax.all_to_all(pack_all(grad_key), 'ctx', split_axis=1, concat_axis=1, ti...  29.7 us
    gather x3, local copies, waits for them, and re-layouts, pack_all(): matrix[safe_found]  16.3 us
    dot_general x1, matrix products, one_block(): jnp.einsum('hqk,khd->qhd', dscores, keys_three, preferred_element_type=jn...  15.9 us
    dot_general x1, matrix products, one_block(): jnp.einsum('hqk,qhd->khd', dscores, query_block, preferred_element_type=j...  14.6 us
    gather x1, local copies, waits for them, and re-layouts, body(): picked_rows = combined[sequence_places]  14.6 us
  transfers between devices with their start and end apart: 4, of which 3 were waited for; matrix products, arithmetic and copies ran while one was open for 13% of the time, Pallas kernels for 0%

commit v1 on v0

v1 whole, which is shorter than its diff:
```python
import functools
import math

import jax
import jax.numpy as jnp
from jax import lax
from jax.experimental import pallas as pl
from jax.experimental.pallas import tpu as pltpu
from jax.sharding import PartitionSpec as P

HEAD_DIM = 128
BF = jnp.bfloat16
F32 = jnp.float32
VMEM_BYTES = 56 * 1024 * 1024


def dot_nn(a, b):
    return lax.dot_general(a, b, (((1,), (0,)), ((), ())), preferred_element_type=F32)


def dot_nt(a, b):
    return lax.dot_general(a, b, (((1,), (1,)), ((), ())), preferred_element_type=F32)


def dot_tn(a, b):
    return lax.dot_general(a, b, (((0,), (0,)), ((), ())), preferred_element_type=F32)


def query_blocks(surv):
    block = 256 if surv % 256 == 0 else surv
    return [(i * block, block) for i in range(surv // block)]


def forward_kernel(q_ref, k_ref, v_ref, probs_ref, out_ref):
    scale = 1.0 / math.sqrt(HEAD_DIM)
    for begin, size in query_blocks(q_ref.shape[0]):
        keys = begin + size
        scores = dot_nt(k_ref[0:keys, :], q_ref[begin:keys, :]) * scale
        key_at = lax.broadcasted_iota(jnp.int32, (keys, size), 0)
        query_at = lax.broadcasted_iota(jnp.int32, (keys, size), 1) + begin
        scores = jnp.where(key_at <= query_at, scores, -jnp.inf)
        exponent = jnp.exp(scores - jnp.max(scores, axis=0, keepdims=True))
        probs = exponent / jnp.sum(exponent, axis=0, keepdims=True)
        probs_ref[0, 0:keys, begin:keys] = probs
        out_ref[begin:keys, :] = dot_tn(probs.astype(BF), v_ref[0:keys, :]).astype(BF)


def forward_heads(q, k, v):
    surv, width = q.shape
    heads = width // HEAD_DIM
    rows = pl.BlockSpec((surv, HEAD_DIM), lambda h: (0, h))
    return pl.pallas_call(
        forward_kernel,
        grid=(heads,),
        in_specs=[rows] * 3,
        out_specs=[pl.BlockSpec((1, surv, surv), lambda h: (h, 0, 0)), rows],
        out_shape=[
            jax.ShapeDtypeStruct((heads, surv, surv), F32),
            jax.ShapeDtypeStruct((surv, width), BF),
        ],
        compiler_params=pltpu.CompilerParams(vmem_limit_bytes=VMEM_BYTES),
        cost_estimate=pl.CostEstimate(
            flops=heads * surv * surv * 600, bytes_accessed=heads * surv * surv * 4,
            transcendentals=heads * surv * surv
        ),
        name="forward_heads",
    )(q, k, v)


def backward_kernel(q_ref, k_ref, v_ref, g_ref, probs_ref, pack_ref, out_ref, gk, gv, joined):
    scale = 1.0 / math.sqrt(HEAD_DIM)
    surv = q_ref.shape[0]
    shards, _, room, _ = out_ref.shape
    gk[...] = jnp.zeros_like(gk)
    gv[...] = jnp.zeros_like(gv)
    for begin, size in query_blocks(surv):
        keys = begin + size
        probs = probs_ref[0, 0:keys, begin:keys]
        grads = g_ref[begin:keys, :]
        dprobs = dot_nt(v_ref[0:keys, :], grads)
        center = jnp.sum(probs * dprobs, axis=0, keepdims=True)
        dscores = (probs * (dprobs - center) * scale).astype(BF)
        joined[begin:keys, 0:HEAD_DIM] = dot_tn(dscores, k_ref[0:keys, :]).astype(BF)
        gk[0:keys, :] += dot_nn(dscores, q_ref[begin:keys, :])
        gv[0:keys, :] += dot_nn(probs.astype(BF), grads)
    joined[:, HEAD_DIM : 2 * HEAD_DIM] = gk[...].astype(BF)
    joined[:, 2 * HEAD_DIM :] = gv[...].astype(BF)
    for shard in range(shards):
        packed = dot_nn(pack_ref[shard * room : (shard + 1) * room, :], joined[...]).astype(BF)
        for part in range(3):
            out_ref[shard, part] = packed[:, part * HEAD_DIM : (part + 1) * HEAD_DIM]


def backward_heads(q, k, v, g, probs, pack, shards):
    surv, width = q.shape
    heads = width // HEAD_DIM
    room = pack.shape[0] // shards
    rows = pl.BlockSpec((surv, HEAD_DIM), lambda h: (0, h))
    return pl.pallas_call(
        backward_kernel,
        grid=(heads,),
        in_specs=[rows] * 4
        + [
            pl.BlockSpec((1, surv, surv), lambda h: (h, 0, 0)),
            pl.BlockSpec(pack.shape, lambda h: (0, 0)),
        ],
        out_specs=pl.BlockSpec((shards, 3, room, HEAD_DIM), lambda h: (0, 0, 0, h)),
        out_shape=jax.ShapeDtypeStruct((shards, 3, room, width), BF),
        scratch_shapes=[
            pltpu.VMEM((surv, HEAD_DIM), F32),
            pltpu.VMEM((surv, HEAD_DIM), F32),
            pltpu.VMEM((surv, 3 * HEAD_DIM), BF),
        ],
        compiler_params=pltpu.CompilerParams(vmem_limit_bytes=VMEM_BYTES),
        cost_estimate=pl.CostEstimate(
            flops=heads * surv * surv * 2000, bytes_accessed=heads * surv * surv * 4,
            transcendentals=0
        ),
        name="backward_heads",
    )(q, k, v, g, probs, pack)


def place_kernel(place_ref, in_ref, out_ref):
    width = in_ref.shape[3]
    for shard in range(in_ref.shape[0]):
        out_ref[:, shard * width : (shard + 1) * width] = dot_nn(
            place_ref[...], in_ref[shard, 0]
        ).astype(BF)


def place_rows(place, received):
    shards, parts, room, width = received.shape
    rows = place.shape[0]
    return pl.pallas_call(
        place_kernel,
        grid=(parts,),
        in_specs=[
            pl.BlockSpec(place.shape, lambda p: (0, 0)),
            pl.BlockSpec((shards, 1, room, width), lambda p: (0, p, 0, 0)),
        ],
        out_specs=pl.BlockSpec((rows, shards * width), lambda p: (0, p)),
        out_shape=jax.ShapeDtypeStruct((rows, parts * shards * width), BF),
        compiler_params=pltpu.CompilerParams(vmem_limit_bytes=VMEM_BYTES),
        name="place_rows",
    )(place, received)


def body(places, grads, projector, queries, keys, values):
    shards = lax.axis_size("ctx")
    me = lax.axis_index("ctx")
    places = places[0]
    surv = places.shape[0]
    rows_here = grads.shape[1]
    room = rows_here * 3 // 4

    edges = jnp.arange(shards + 1, dtype=jnp.int32) * rows_here
    first = jnp.sum((places[None, :] < edges[:, None]).astype(jnp.int32), axis=1)
    slot = jnp.arange(room, dtype=jnp.int32)
    rank = first[:-1, None] + slot[None, :]
    rank = jnp.where(rank < first[1:, None], rank, -1).reshape(-1)
    pack = (rank[:, None] == jnp.arange(surv, dtype=jnp.int32)[None, :]).astype(BF)

    mine = lax.dynamic_slice_in_dim(rank, me * room, room)
    hit = mine[:, None] == jnp.arange(surv, dtype=jnp.int32)[None, :]
    local = jnp.sum(jnp.where(hit, places[None, :] - me * rows_here + 1, 0), axis=1) - 1
    row = jnp.arange(rows_here, dtype=jnp.int32)
    place = (row[:, None] == local[None, :]).astype(BF)
    compact = (local[:, None] == row[None, :]).astype(BF)

    sent = dot_nn(compact, grads[0]).astype(BF)
    gathered = lax.all_gather(sent, "ctx", axis=0, tiled=True)

    q, k, v = queries[0], keys[0], values[0]
    probs, outputs = forward_heads(q, k, v)
    outputs = dot_nn(pack, outputs).astype(BF)

    partial = dot_tn(outputs, gathered).astype(BF)
    projector_derivative = lax.psum(partial, "dp").astype(F32)

    slot_grads = dot_nt(gathered, projector).astype(BF)
    head_grads = dot_tn(pack, slot_grads).astype(BF)
    packed = backward_heads(q, k, v, head_grads, probs, pack, shards)
    received = lax.all_to_all(packed, "ctx", split_axis=0, concat_axis=0, tiled=True)
    every_place = place_rows(place, received)
    return (every_place[None], projector_derivative)


def solution(mesh):
    in_specs = (
        P("dp", None),
        P("dp", "ctx", None),
        P("ctx", None),
        P("dp", None, "ctx"),
        P("dp", None, "ctx"),
        P("dp", None, "ctx"),
    )
    out_specs = (P("dp", "ctx", None), P("ctx", None))
    return jax.shard_map(body, mesh=mesh, in_specs=in_specs, out_specs=out_specs, check_vma=False)
```

time: 387 us -> 210 us (0.54)
  local copies, waits for them, and re-layouts: 62.2 us -> 0.41 us
  matrix products: 68.4 us -> 19.1 us
  blocking collectives: 40 us -> 0 us
  Pallas kernels: 0 us -> 29.1 us
  waiting for transfers between devices: 159 us -> 130 us
  other arithmetic: 25.8 us -> 8.33 us
  starting transfers between devices: 15.2 us -> 6.82 us
    dot_general x7 -> x3, matrix products: 60 us -> 19.1 us  [the longest x2 16.6 us: dot_tn(): lax.dot_general(a, b, (((0,), (0,)), ((), ())), preferred_element_type=F32)]
    all_to_all x1 -> x0, blocking collectives: 40 us -> none  [body(): lax.all_to_all(pack_all(grad_query), 'ctx', split_axis=1, concat_axis=1,...]
    gather x5 -> x0, local copies, waits for them, and re-layouts: 39.2 us -> none  [the longest x3 16.3 us: pack_all(): matrix[safe_found]]
    all_to_all x2 -> x1, waiting for transfers between devices: 29.7 us -> 0.01 us  [body(): lax.all_to_all(packed, 'ctx', split_axis=0, concat_axis=0, tiled=True)]
    pallas_call x0 -> x3, Pallas kernels: none -> 29.1 us  [the longest x1 15.1 us: backward_heads(): pl.pallas_call(backward_kernel, grid=(heads,), in_specs=[rows] * 4 + [pl....]
    reshape x5 -> x0, local copies, waits for them, and re-layouts: 9.58 us -> none  [the longest x3 5.87 us: body(): part_grad.reshape(rows_here, shard_count * local_width)]
    concatenate x1 -> x0, other arithmetic: 8.73 us -> none  [project(): return jnp.concatenate([portion, products.astype(jnp.bfloat16)], axis=1)]
    sub x1 -> x0, matrix products: 8.4 us -> none  [one_block(): exponent = jnp.exp(scores - row_max)]
  transfers between devices with their start and end apart: 4 -> 3, of which waited for: 3 -> 2; matrix products, arithmetic and copies ran while one was open for 13% -> 8% of each run, Pallas kernels for 0% -> 4%
where the time goes in v1:
time: 210 us; the launch traced here: 208 us
  waiting for transfers between devices  130 us (62%)
  Pallas kernels  29.1 us (14%)
  matrix products  19.1 us (9%)
  between operations  14.1 us (7%)
  other arithmetic  8.33 us (4%)
  starting transfers between devices  6.82 us (3%)
    psum x1, waiting for transfers between devices, body(): projector_derivative = lax.psum(partial, 'dp').astype(F32)  78.5 us
    all_gather x1, waiting for transfers between devices, body(): gathered = lax.all_gather(sent, 'ctx', axis=0, tiled=True)  51.5 us
    dot_general x2, matrix products, dot_tn(): lax.dot_general(a, b, (((0,), (0,)), ((), ())), preferred_element_type=F32)  16.6 us
    pallas_call x1, Pallas kernels, backward_heads(): pl.pallas_call(backward_kernel, grid=(heads,), in_specs=[rows] * 4 + [pl....  15.1 us
    pallas_call x1, Pallas kernels, forward_heads(): pl.pallas_call(forward_kernel, grid=(heads,), in_specs=[rows] * 3, out_sp...  8.31 us
    all_to_all x1, starting transfers between devices, body(): lax.all_to_all(packed, 'ctx', split_axis=0, concat_axis=0, tiled=True)  6.78 us
    pallas_call x1, Pallas kernels, place_rows(): pl.pallas_call(place_kernel, grid=(parts,), in_specs=[pl.BlockSpec(place....  5.7 us
    convert_element_type x1, other arithmetic, body(): projector_derivative = lax.psum(partial, 'dp').astype(F32)  4.78 us
  transfers between devices with their start and end apart: 3, of which 2 were waited for; matrix products, arithmetic and copies ran while one was open for 8% of the time, Pallas kernels for 4%

profile of v1, /device:TPU:11, one launch (start us, length us, event | category | flops | bytes accessed | tf_op | source)
XLA Modules:
  0.0 207.9 jit_solution(7567789078288990825)
XLA Ops:
  7.2 0.0 copy-start
  7.2 0.0 all-gather.2.cloned.1.call-start
  7.2 0.9 fusion.10
  8.1 0.2 convert_reduce_fusion
  8.3 0.1 fusion.11
  8.4 0.1 lt.37
  8.4 0.1 lt.38
  8.5 0.1 iota_add_fusion
  8.6 0.1 add.44
  8.7 0.1 dynamic_slice.3
  8.8 0.2 select_reduce_fusion
  9.0 2.5 %convolution_convert_fusion.1 = bf16[144,2560]{1,0:T(8,128)(2,1)} fusion(bf16[1,192,2560]{2,1,0:T(8,128)(2,1)} %param.7, s32[144]{0:T(256)S(1)} %broadcast_add_fusion), kind=kOutput, calls=%fused_computation.1 | convolution fusion | flops 141954048 | bytes 1720896 | tf_op jit(solution)/shard_map/dot_general | solution.py:18
  11.5 0.0 all-gather.2.cloned.1.call-update
  11.5 8.3 %forward_heads.1 = (f32[4,768,768]{2,1,0:T(8,128)}, bf16[768,512]{1,0:T(8,128)(2,1)}) custom-call(bf16[768,512]{1,0:T(8,128)(2,1)} %bitcast.12, bf16[768,512]{1,0:T(8,128)(2,1)} %bitcast.14, bf16[768,512]{1,0:T(8,128)(2,1)} %bitcast.16), custom_call_target="tpu_custom_call" | custom-call | flops 1415577600 | bytes 9437184 | tf_op jit(solution)/shard_map/forward_heads/pallas_call | solution.py:52
  19.8 1.6 fusion.1.pack_ref
  21.4 51.5 %all-gather.2.cloned.1.call-done = bf16[1152,2560]{1,0:T(8,128)(2,1)} async-done(((bf16[144,2560]{1,0:T(8,128)(2,1)}), bf16[1152,2560]{1,0:T(8,128)(2,1)}) %all-gather.2.cloned.1.call-update) | async-done | bytes 5898256 | tf_op jit(solution)/shard_map/all_gather | solution.py:171
  72.9 0.0 copy-done
  72.9 7.8 %fusion.6.g_ref = bf16[768,512]{1,0:T(8,128)(2,1)} fusion(s32[1152]{0:T(1024)S(1)} %compare_select_fusion, bf16[1152,2560]{1,0:T(8,128)(2,1)} %all-gather.2.cloned.1.call-done, bf16[512,2560]{1,0:T(8,128)(2,1)S(1)} %copy-done), kind=kOutput, calls=%fused_computation.10 | convolution fusion | flops 3927736320 | bytes 9310720 | tf_op jit(solution)/shard_map/dot_general | solution.py:26
  80.7 15.1 %backward_heads.1 = bf16[8,3,144,512]{3,2,1,0:T(8,128)(2,1)} custom-call(bf16[768,512]{1,0:T(8,128)(2,1)} %bitcast.13, bf16[768,512]{1,0:T(8,128)(2,1)} %bitcast.15, bf16[768,512]{1,0:T(8,128)(2,1)} %bitcast.17, bf16[768,512]{1,0:T(8,128)(2,1)} %fusion.6.g_ref, f32[4,768,768]{2,1,0:T(8,128)} %get-tuple-element.4.probs_ref, bf16[1152,768]{1,0:T(8,128)(2,1)} %fusion.1.pack_ref), custom_call_target="tpu_custom_call" | custom-call | flops 4718592000 | bytes 9437184 | tf_op jit(solution)/shard_map/backward_heads/pallas_call | solution.py:99
  95.8 0.0 copy-start.1
  95.8 6.8 %all-to-all-start = ((bf16[8,3,144,512]{3,2,1,0:T(8,128)(2,1)}), bf16[8,3,144,512]{3,2,1,0:T(8,128)(2,1)}, u32[]{:S(2)}, u32[]{:S(2)}) async-start(bf16[8,3,144,512]{3,2,1,0:T(8,128)(2,1)} %backward_heads.1), calls=%async_computation | async-start | bytes 7077888 | tf_op jit(solution)/shard_map/all_to_all | solution.py:183
  102.6 0.0 all-reduce.2.cloned.1.call-start
  102.6 0.0 copy-done.1
  102.6 8.8 %convolution_convert_fusion = bf16[512,2560]{1,0:T(8,128)(2,1)} fusion(bf16[1152,2560]{1,0:T(8,128)(2,1)} %all-gather.2.cloned.1.call-done, bf16[768,512]{1,0:T(8,128)(2,1)S(1)} %copy-done.1, s32[1152]{0:T(1024)S(1)} %compare_select_fusion), kind=kOutput, calls=%fused_computation | convolution fusion | flops 3928653824 | bytes 9310720 | tf_op jit(solution)/shard_map/dot_general | solution.py:26
  111.4 0.0 all-reduce.2.cloned.1.call-update
  111.4 0.7 fusion.8.place_ref
  112.1 78.5 %all-reduce.2.cloned.1.call-done = bf16[512,2560]{1,0:T(8,128)(2,1)} async-done(((bf16[512,2560]{1,0:T(8,128)(2,1)}), bf16[512,2560]{1,0:T(8,128)(2,1)}) %all-reduce.2.cloned.1.call-update) | async-done | bytes 2621456 | tf_op jit(solution)/shard_map/psum | solution.py:178
  190.6 4.8 %convert_element_type.36 = f32[512,2560]{1,0:T(8,128)} convert(bf16[512,2560]{1,0:T(8,128)(2,1)} %all-reduce.2.cloned.1.call-done) | non-fusion elementwise | flops 1310720 | bytes 7864320 | tf_op jit(solution)/shard_map/convert_element_type | solution.py:178
  195.4 0.0 all-to-all-done.in_ref
  195.4 5.7 %place_rows.1 = bf16[192,12288]{1,0:T(8,128)(2,1)} custom-call(bf16[192,144]{1,0:T(8,128)(2,1)} %fusion.8.place_ref, bf16[8,3,144,512]{3,2,1,0:T(8,128)(2,1)} %all-to-all-done.in_ref), custom_call_target="tpu_custom_call" | custom-call | tf_op jit(solution)/shard_map/place_rows/pallas_call | solution.py:134
  (3 shorter events, 0.0 us)
Async XLA Ops:
  7.2 65.7 %copy-start = (bf16[512,2560]{1,0:T(8,128)(2,1)S(1)}, bf16[512,2560]{1,0:T(8,128)(2,1)}, u32[]{:S(2)}) copy-start(bf16[512,2560]{1,0:T(8,128)(2,1)} %param.8) | copy-start | bytes 7864324
  7.2 65.7 %all-gather.2.cloned.1.call-start = ((), (), s32[]{:S(2)}) async-start(), calls=%async_computation.1 | async-start | bytes 6635520 | tf_op jit(solution)/shard_map/all_gather | solution.py:171
  95.8 6.8 %copy-start.1 = (bf16[768,512]{1,0:T(8,128)(2,1)S(1)}, bf16[768,512]{1,0:T(8,128)(2,1)}, u32[]{:S(2)}) copy-start(bf16[768,512]{1,0:T(8,128)(2,1)} %get-tuple-element.5) | copy-start | bytes 2359300
  95.8 99.5 %all-to-all-start = ((bf16[8,3,144,512]{3,2,1,0:T(8,128)(2,1)}), bf16[8,3,144,512]{3,2,1,0:T(8,128)(2,1)}, u32[]{:S(2)}, u32[]{:S(2)}) async-start(bf16[8,3,144,512]{3,2,1,0:T(8,128)(2,1)} %backward_heads.1), calls=%async_computation | async-start | bytes 7077888 | tf_op jit(solution)/shard_map/all_to_all | solution.py:183
  102.6 88.0 %all-reduce.2.cloned.1.call-start = ((), (), s32[]{:S(2)}) async-start(), calls=%async_computation.2 | async-start | bytes 5242880 | tf_op jit(solution)/shard_map/psum | solution.py:178
Sparse Core Ops, SparseCore 0:
  11.6 61.2 all-gather.1
  111.6 78.9 all-reduce.1

commit v2 on v1

--- a/solution.py
+++ b/solution.py
@@ -67,10 +67,48 @@
     )(q, k, v)
 
 
-def backward_kernel(q_ref, k_ref, v_ref, g_ref, probs_ref, pack_ref, out_ref, gk, gv, joined):
+def backward_kernel(
+    q_ref, k_ref, v_ref, g_ref, probs_ref, pack_ref, recv_ref, gk, gv, joined, outbox, send_sem, recv_sem, own_sem
+):
+    head = pl.program_id(0)
+    heads, shards, _, room, _ = outbox.shape
+    me, group = lax.axis_index("ctx"), lax.axis_index("dp")
+    peers = [lax.rem(me + offset, shards) for offset in range(1, shards)]
+
+    @pl.when(head == 0)
+    def _():
+        barrier = pltpu.get_barrier_semaphore()
+        for peer in peers:
+            pl.semaphore_signal(
+                barrier, inc=1, device_id=(group, peer), device_id_type=pl.DeviceIdType.MESH
+            )
+        pl.semaphore_wait(barrier, shards - 1)
+
+    def outgoing(h, peer):
+        return pltpu.make_async_remote_copy(
+            src_ref=outbox.at[h, peer],
+            dst_ref=recv_ref.at[me, h],
+            send_sem=send_sem.at[h, peer],
+            recv_sem=recv_sem.at[h, me],
+            device_id=(group, peer),
+            device_id_type=pl.DeviceIdType.MESH,
+        )
+
+    def incoming(h, peer):
+        return pltpu.make_async_remote_copy(
+            src_ref=outbox.at[h, peer],
+            dst_ref=recv_ref.at[peer, h],
+            send_sem=send_sem.at[h, peer],
+            recv_sem=recv_sem.at[h, peer],
+            device_id=(group, peer),
+            device_id_type=pl.DeviceIdType.MESH,
+        )
+
+    def own(h):
+        return pltpu.make_async_copy(outbox.at[h, me], recv_ref.at[me, h], own_sem.at[h])
+
     scale = 1.0 / math.sqrt(HEAD_DIM)
     surv = q_ref.shape[0]
-    shards, _, room, _ = out_ref.shape
     gk[...] = jnp.zeros_like(gk)
     gv[...] = jnp.zeros_like(gv)
     for begin, size in query_blocks(surv):
@@ -85,10 +123,24 @@
         gv[0:keys, :] += dot_nn(probs.astype(BF), grads)
     joined[:, HEAD_DIM : 2 * HEAD_DIM] = gk[...].astype(BF)
     joined[:, 2 * HEAD_DIM :] = gv[...].astype(BF)
-    for shard in range(shards):
-        packed = dot_nn(pack_ref[shard * room : (shard + 1) * room, :], joined[...]).astype(BF)
+
+    for peer in peers + [me]:
+        slots = pl.ds(pl.multiple_of(peer * room, 16), room)
+        packed = dot_nn(pack_ref[slots, :], joined[...]).astype(BF)
         for part in range(3):
-            out_ref[shard, part] = packed[:, part * HEAD_DIM : (part + 1) * HEAD_DIM]
+            outbox[head, peer, part] = packed[:, part * HEAD_DIM : (part + 1) * HEAD_DIM]
+        if peer is me:
+            own(head).start()
+        else:
+            outgoing(head, peer).start()
+
+    @pl.when(head == heads - 1)
+    def _():
+        for h in range(heads):
+            own(h).wait()
+            for peer in peers:
+                outgoing(h, peer).wait_send()
+                incoming(h, peer).wait_recv()
 
 
 def backward_heads(q, k, v, g, probs, pack, shards):
@@ -104,16 +156,22 @@
             pl.BlockSpec((1, surv, surv), lambda h: (h, 0, 0)),
             pl.BlockSpec(pack.shape, lambda h: (0, 0)),
         ],
-        out_specs=pl.BlockSpec((shards, 3, room, HEAD_DIM), lambda h: (0, 0, 0, h)),
-        out_shape=jax.ShapeDtypeStruct((shards, 3, room, width), BF),
+        out_specs=pl.BlockSpec(memory_space=pl.ANY),
+        out_shape=jax.ShapeDtypeStruct((shards, heads, 3, room, HEAD_DIM), BF),
         scratch_shapes=[
             pltpu.VMEM((surv, HEAD_DIM), F32),
             pltpu.VMEM((surv, HEAD_DIM), F32),
             pltpu.VMEM((surv, 3 * HEAD_DIM), BF),
-        ],
-        compiler_params=pltpu.CompilerParams(vmem_limit_bytes=VMEM_BYTES),
+            pltpu.VMEM((heads, shards, 3, room, HEAD_DIM), BF),
+            pltpu.SemaphoreType.DMA((heads, shards)),
+            pltpu.SemaphoreType.DMA((heads, shards)),
+            pltpu.SemaphoreType.DMA((heads,)),
+        ],
+        compiler_params=pltpu.CompilerParams(
+            vmem_limit_bytes=VMEM_BYTES, collective_id=0, has_side_effects=True
+        ),
         cost_estimate=pl.CostEstimate(
-            flops=heads * surv * surv * 2000, bytes_accessed=heads * surv * surv * 4,
+            flops=heads * surv * surv * 20000, bytes_accessed=heads * surv * surv * 4,
             transcendentals=0
         ),
         name="backward_heads",
@@ -121,25 +179,26 @@
 
 
 def place_kernel(place_ref, in_ref, out_ref):
-    width = in_ref.shape[3]
-    for shard in range(in_ref.shape[0]):
-        out_ref[:, shard * width : (shard + 1) * width] = dot_nn(
-            place_ref[...], in_ref[shard, 0]
-        ).astype(BF)
+    shards, heads, _, _, dim = in_ref.shape
+    width = heads * dim
+    for shard in range(shards):
+        held = jnp.concatenate([in_ref[shard, h, 0] for h in range(heads)], axis=1)
+        out_ref[:, shard * width : (shard + 1) * width] = dot_nn(place_ref[...], held).astype(BF)
 
 
 def place_rows(place, received):
-    shards, parts, room, width = received.shape
+    shards, heads, parts, room, dim = received.shape
     rows = place.shape[0]
+    width = shards * heads * dim
     return pl.pallas_call(
         place_kernel,
         grid=(parts,),
         in_specs=[
             pl.BlockSpec(place.shape, lambda p: (0, 0)),
-            pl.BlockSpec((shards, 1, room, width), lambda p: (0, p, 0, 0)),
-        ],
-        out_specs=pl.BlockSpec((rows, shards * width), lambda p: (0, p)),
-        out_shape=jax.ShapeDtypeStruct((rows, parts * shards * width), BF),
+            pl.BlockSpec((shards, heads, 1, room, dim), lambda p: (0, 0, p, 0, 0)),
+        ],
+        out_specs=pl.BlockSpec((rows, width), lambda p: (0, p)),
+        out_shape=jax.ShapeDtypeStruct((rows, parts * width), BF),
         compiler_params=pltpu.CompilerParams(vmem_limit_bytes=VMEM_BYTES),
         name="place_rows",
     )(place, received)
@@ -177,10 +236,10 @@
     partial = dot_tn(outputs, gathered).astype(BF)
     projector_derivative = lax.psum(partial, "dp").astype(F32)
 
+    gathered, _ = lax.optimization_barrier((gathered, partial))
     slot_grads = dot_nt(gathered, projector).astype(BF)
     head_grads = dot_tn(pack, slot_grads).astype(BF)
-    packed = backward_heads(q, k, v, head_grads, probs, pack, shards)
-    received = lax.all_to_all(packed, "ctx", split_axis=0, concat_axis=0, tiled=True)
+    received = backward_heads(q, k, v, head_grads, probs, pack, shards)
     every_place = place_rows(place, received)
     return (every_place[None], projector_derivative)
 

time: 210 us -> 194 us (0.924)
  waiting for transfers between devices: 130 us -> 50.7 us
  Pallas kernels: 29.1 us -> 101 us
  starting transfers between devices: 6.82 us -> 0.08 us
    psum x1, waiting for transfers between devices: 78.5 us -> 0.01 us  [body(): projector_derivative = lax.psum(partial, 'dp').astype(F32)]
    pallas_call x1, Pallas kernels: 15.1 us -> 86.5 us  [backward_heads(): pl.pallas_call(backward_kernel, grid=(heads,), in_specs=[rows] * 4 + [pl....]
    all_to_all x1 -> x0, starting transfers between devices: 6.78 us -> none  [body(): lax.all_to_all(packed, 'ctx', split_axis=0, concat_axis=0, tiled=True)]
  transfers between devices with their start and end apart: 3 -> 2, of which waited for: 2 -> 1; matrix products, arithmetic and copies ran while one was open for 8% -> 5% of each run, Pallas kernels for 4% -> 52%
where the time goes in v2:
time: 194 us
  Pallas kernels  101 us (52%)
  waiting for transfers between devices  50.7 us (26%)
  matrix products  19.4 us (10%)
  between operations  14.1 us (7%)
  other arithmetic  8.33 us (4%)
    pallas_call x1, Pallas kernels, backward_heads(): pl.pallas_call(backward_kernel, grid=(heads,), in_specs=[rows] * 4 + [pl....  86.5 us
    all_gather x1, waiting for transfers between devices, body(): gathered = lax.all_gather(sent, 'ctx', axis=0, tiled=True)  50.6 us
    dot_general x2, matrix products, dot_tn(): lax.dot_general(a, b, (((0,), (0,)), ((), ())), preferred_element_type=F32)  16.9 us
    pallas_call x1, Pallas kernels, forward_heads(): pl.pallas_call(forward_kernel, grid=(heads,), in_specs=[rows] * 3, out_sp...  8.31 us
    pallas_call x1, Pallas kernels, place_rows(): pl.pallas_call(place_kernel, grid=(parts,), in_specs=[pl.BlockSpec(place....  5.74 us
    convert_element_type x1, other arithmetic, body(): projector_derivative = lax.psum(partial, 'dp').astype(F32)  4.78 us
  transfers between devices with their start and end apart: 2, of which 1 were waited for; matrix products, arithmetic and copies ran while one was open for 5% of the time, Pallas kernels for 52%

profile of v2, /device:TPU:11, one launch (start us, length us, event | category | flops | bytes accessed | tf_op | source)
XLA Modules:
  0.0 193.5 jit_solution(15986422764275434251)
XLA Ops:
  7.2 0.0 copy-start
  7.2 0.0 all-gather.2.cloned.1.call-start
  7.2 0.9 fusion.10
  8.1 0.2 convert_reduce_fusion
  8.3 0.1 fusion.11
  8.4 0.1 iota_add_fusion
  8.4 0.1 add.44
  8.5 0.1 lt.37
  8.6 0.1 lt.38
  8.7 0.1 dynamic_slice.3
  8.8 0.2 select_reduce_fusion
  9.0 2.5 %convolution_convert_fusion.1 = bf16[144,2560]{1,0:T(8,128)(2,1)} fusion(bf16[1,192,2560]{2,1,0:T(8,128)(2,1)} %param.7, s32[144]{0:T(256)S(1)} %broadcast_add_fusion), kind=kOutput, calls=%fused_computation.1 | convolution fusion | flops 141954048 | bytes 1720896 | tf_op jit(solution)/shard_map/dot_general | solution.py:18
  11.5 0.0 all-gather.2.cloned.1.call-update
  11.5 0.0 all-reduce.2.cloned.1.call-start
  11.5 8.3 %forward_heads.1 = (f32[4,768,768]{2,1,0:T(8,128)}, bf16[768,512]{1,0:T(8,128)(2,1)}) custom-call(bf16[768,512]{1,0:T(8,128)(2,1)} %bitcast.12, bf16[768,512]{1,0:T(8,128)(2,1)} %bitcast.14, bf16[768,512]{1,0:T(8,128)(2,1)} %bitcast.16), custom_call_target="tpu_custom_call" | custom-call | flops 1415577600 | bytes 9437184 | tf_op jit(solution)/shard_map/forward_heads/pallas_call | solution.py:52
  19.9 0.7 fusion.8.place_ref
  20.5 1.6 fusion.pack_ref
  22.1 50.6 %all-gather.2.cloned.1.call-done = bf16[1152,2560]{1,0:T(8,128)(2,1)} async-done(((bf16[144,2560]{1,0:T(8,128)(2,1)}), bf16[1152,2560]{1,0:T(8,128)(2,1)}) %all-gather.2.cloned.1.call-update) | async-done | bytes 5898256 | tf_op jit(solution)/shard_map/all_gather | solution.py:230
  72.7 9.0 %convolution_convert_fusion = bf16[512,2560]{1,0:T(8,128)(2,1)} fusion(bf16[1152,2560]{1,0:T(8,128)(2,1)} %all-gather.2.cloned.1.call-done, bf16[768,512]{1,0:T(8,128)(2,1)} %get-tuple-element.5, s32[1152]{0:T(1024)S(1)} %compare_select_fusion), kind=kOutput, calls=%fused_computation | convolution fusion | flops 3928653824 | bytes 9310720 | tf_op jit(solution)/shard_map/dot_general | solution.py:26
  81.7 0.0 all-reduce.2.cloned.1.call-update
  81.8 0.0 copy-done
  81.8 7.9 %fusion.6.g_ref = bf16[768,512]{1,0:T(8,128)(2,1)} fusion(s32[1152]{0:T(1024)S(1)} %compare_select_fusion, bf16[1152,2560]{1,0:T(8,128)(2,1)} %all-gather.2.cloned.1.call-done, bf16[512,2560]{1,0:T(8,128)(2,1)S(1)} %copy-done), kind=kOutput, calls=%fused_computation.10 | convolution fusion | flops 3927736320 | bytes 9310720 | tf_op jit(solution)/shard_map/dot_general | solution.py:26
  89.6 86.5 %backward_heads.1.in_ref = bf16[8,4,3,144,128]{4,3,2,1,0:T(8,128)(2,1)} custom-call(bf16[768,512]{1,0:T(8,128)(2,1)} %bitcast.13, bf16[768,512]{1,0:T(8,128)(2,1)} %bitcast.15, bf16[768,512]{1,0:T(8,128)(2,1)} %bitcast.17, bf16[768,512]{1,0:T(8,128)(2,1)} %fusion.6.g_ref, f32[4,768,768]{2,1,0:T(8,128)} %get-tuple-element.7.probs_ref, ...), custom_call_target="tpu_custom_call" | custom-call | flops 47185920000 | bytes 9437184 | tf_op jit(solution)/shard_map/backward_heads/pallas_call | solution.py:151
  176.2 5.7 %place_rows.1 = bf16[192,12288]{1,0:T(8,128)(2,1)} custom-call(bf16[192,144]{1,0:T(8,128)(2,1)} %fusion.8.place_ref, bf16[8,4,3,144,128]{4,3,2,1,0:T(8,128)(2,1)} %backward_heads.1.in_ref), custom_call_target="tpu_custom_call" | custom-call | tf_op jit(solution)/shard_map/place_rows/pallas_call | solution.py:193
  181.9 0.0 all-reduce.2.cloned.1.call-done
  181.9 4.8 %convert_element_type.36 = f32[512,2560]{1,0:T(8,128)} convert(bf16[512,2560]{1,0:T(8,128)(2,1)} %all-reduce.2.cloned.1.call-done) | non-fusion elementwise | flops 1310720 | bytes 7864320 | tf_op jit(solution)/shard_map/convert_element_type | solution.py:237
  (3 shorter events, 0.0 us)
Async XLA Ops:
  7.2 74.6 %copy-start = (bf16[512,2560]{1,0:T(8,128)(2,1)S(1)}, bf16[512,2560]{1,0:T(8,128)(2,1)}, u32[]{:S(2)}) copy-start(bf16[512,2560]{1,0:T(8,128)(2,1)} %param.8) | copy-start | bytes 7864324
  7.2 65.5 %all-gather.2.cloned.1.call-start = ((), (), s32[]{:S(2)}) async-start(), calls=%async_computation | async-start | bytes 6635520 | tf_op jit(solution)/shard_map/all_gather | solution.py:230
  11.5 170.4 %all-reduce.2.cloned.1.call-start = ((), (), s32[]{:S(2)}) async-start(), calls=%async_computation.1 | async-start | bytes 5242880 | tf_op jit(solution)/shard_map/psum | solution.py:237
Sparse Core Ops, SparseCore 0:
  11.6 61.0 all-gather.1
  81.9 78.7 all-reduce.1

commit v3 on v2

--- a/solution.py
+++ b/solution.py
@@ -31,40 +31,211 @@
     return [(i * block, block) for i in range(surv // block)]
 
 
-def forward_kernel(q_ref, k_ref, v_ref, probs_ref, out_ref):
+def gather_kernel(
+    compact_ref, grads_ref, w_ref, pack_ref, q_ref, k_ref, v_ref,
+    probs_ref, head_grads_ref, partial_ref,
+    blocks, stage, outputs, slot_outputs, slot_grads, total, send_sem, recv_sem, stage_sem,
+):
+    shards, room, _ = blocks.shape
+    surv, width = q_ref.shape
+    heads = width // HEAD_DIM
+    me, group = lax.axis_index("ctx"), lax.axis_index("dp")
+    chips = shards // 2
+    chip, core = me // 2, me % 2
+    other = chip * 2 + (1 - core)
+    after, before = lax.rem(me + 2, shards), lax.rem(me + shards - 2, shards)
+
+    blocks[me] = dot_nn(compact_ref[...], grads_ref[...]).astype(BF)
+
+    barrier = pltpu.get_barrier_semaphore()
+    for offset in range(1, shards):
+        pl.semaphore_signal(
+            barrier, inc=1, device_id=(group, lax.rem(me + offset, shards)),
+            device_id_type=pl.DeviceIdType.MESH,
+        )
+    pl.semaphore_wait(barrier, shards - 1)
+
+    def hop(slot, way, target):
+        return pltpu.make_async_remote_copy(
+            src_ref=blocks.at[slot],
+            dst_ref=blocks.at[slot],
+            send_sem=send_sem.at[way, slot],
+            recv_sem=recv_sem.at[slot],
+            device_id=(group, target),
+            device_id_type=pl.DeviceIdType.MESH,
+        )
+
+    def up(slot):
+        return hop(slot, 0, after)
+
+    def down(slot):
+        return hop(slot, 1, before)
+
+    def across(slot):
+        return hop(slot, 2, other)
+
+    @pl.when(chip < chips - 1)
+    def _():
+        up(me).start()
+
+    @pl.when(chip > 0)
+    def _():
+        down(me).start()
+
+    across(me).start()
+
     scale = 1.0 / math.sqrt(HEAD_DIM)
-    for begin, size in query_blocks(q_ref.shape[0]):
-        keys = begin + size
-        scores = dot_nt(k_ref[0:keys, :], q_ref[begin:keys, :]) * scale
-        key_at = lax.broadcasted_iota(jnp.int32, (keys, size), 0)
-        query_at = lax.broadcasted_iota(jnp.int32, (keys, size), 1) + begin
-        scores = jnp.where(key_at <= query_at, scores, -jnp.inf)
-        exponent = jnp.exp(scores - jnp.max(scores, axis=0, keepdims=True))
-        probs = exponent / jnp.sum(exponent, axis=0, keepdims=True)
-        probs_ref[0, 0:keys, begin:keys] = probs
-        out_ref[begin:keys, :] = dot_tn(probs.astype(BF), v_ref[0:keys, :]).astype(BF)
-
-
-def forward_heads(q, k, v):
+
+    def keep(head):
+        return pltpu.make_async_copy(stage, probs_ref.at[head], stage_sem)
+
+    def forward(head, carry):
+        lanes = pl.ds(pl.multiple_of(head * HEAD_DIM, HEAD_DIM), HEAD_DIM)
+
+        @pl.when(head > 0)
+        def _():
+            keep(head - 1).wait()
+
+        for begin, size in query_blocks(surv):
+            keys = begin + size
+            scores = dot_nt(k_ref[0:keys, lanes], q_ref[begin:keys, lanes]) * scale
+            key_at = lax.broadcasted_iota(jnp.int32, (keys, size), 0)
+            query_at = lax.broadcasted_iota(jnp.int32, (keys, size), 1) + begin
+            scores = jnp.where(key_at <= query_at, scores, -jnp.inf)
+            exponent = jnp.exp(scores - jnp.max(scores, axis=0, keepdims=True))
+            probs = exponent / jnp.sum(exponent, axis=0, keepdims=True)
+            stage[0:keys, begin:keys] = probs
+            outputs[begin:keys, lanes] = dot_tn(probs.astype(BF), v_ref[0:keys, lanes]).astype(BF)
+        keep(head).start()
+        return carry
+
+    lax.fori_loop(0, heads, forward, 0)
+    slot_outputs[...] = dot_nn(pack_ref[...], outputs[...]).astype(BF)
+    keep(heads - 1).wait()
+
+    def work(slot):
+        rows = pl.ds(pl.multiple_of(slot * room, 16), room)
+        slot_grads[rows, :] = dot_nt(blocks[slot], w_ref[...]).astype(BF)
+        total[...] += dot_tn(slot_outputs[rows, :], blocks[slot])
+
+    total[...] = jnp.zeros_like(total)
+    work(me)
+    across(other).wait_recv()
+    work(other)
+
+    def step(distance, carry):
+        lower, upper = chip - distance, chip + distance
+
+        @pl.when(lower >= 0)
+        def _():
+            slot = lower * 2 + core
+            up(slot).wait_recv()
+
+            @pl.when(chip < chips - 1)
+            def _():
+                up(slot).start()
+
+            across(slot).start()
+
+        @pl.when(upper < chips)
+        def _():
+            slot = upper * 2 + core
+            down(slot).wait_recv()
+
+            @pl.when(chip > 0)
+            def _():
+                down(slot).start()
+
+            across(slot).start()
+
+        def each(which, inner):
+            source = chip + (2 * (which % 2) - 1) * distance
+            from_other = which // 2
+            slot = source * 2 + core + from_other * (1 - 2 * core)
+
+            @pl.when((source >= 0) & (source < chips))
+            def _():
+                @pl.when(from_other == 1)
+                def _():
+                    across(slot).wait_recv()
+
+                work(slot)
+
+            return inner
+
+        lax.fori_loop(0, 4, each, 0)
+        return carry
+
+    lax.fori_loop(1, chips, step, 0)
+
+    head_grads_ref[...] = dot_tn(pack_ref[...], slot_grads[...]).astype(BF)
+    partial_ref[...] = total[...].astype(BF)
+
+    across(me).wait_send()
+
+    @pl.when(chip < chips - 1)
+    def _():
+        up(me).wait_send()
+
+    @pl.when(chip > 0)
+    def _():
+        down(me).wait_send()
+
+    def finish(distance, carry):
+        lower, upper = chip - distance, chip + distance
+
+        @pl.when(lower >= 0)
+        def _():
+            across(lower * 2 + core).wait_send()
+
+            @pl.when(chip < chips - 1)
+            def _():
+                up(lower * 2 + core).wait_send()
+
+        @pl.when(upper < chips)
+        def _():
+            across(upper * 2 + core).wait_send()
+
+            @pl.when(chip > 0)
+            def _():
+                down(upper * 2 + core).wait_send()
+
+        return carry
+
+    lax.fori_loop(1, chips, finish, 0)
+
+
+def gather_forward(compact, grads, w, pack, q, k, v, shards):
     surv, width = q.shape
     heads = width // HEAD_DIM
-    rows = pl.BlockSpec((surv, HEAD_DIM), lambda h: (0, h))
+    room = compact.shape[0]
+    model = grads.shape[1]
+    whole = pl.BlockSpec(memory_space=pltpu.VMEM)
     return pl.pallas_call(
-        forward_kernel,
-        grid=(heads,),
-        in_specs=[rows] * 3,
-        out_specs=[pl.BlockSpec((1, surv, surv), lambda h: (h, 0, 0)), rows],
+        gather_kernel,
+        in_specs=[whole] * 7,
+        out_specs=[pl.BlockSpec(memory_space=pl.ANY), whole, whole],
         out_shape=[
             jax.ShapeDtypeStruct((heads, surv, surv), F32),
             jax.ShapeDtypeStruct((surv, width), BF),
+            jax.ShapeDtypeStruct((width, model), BF),
         ],
-        compiler_params=pltpu.CompilerParams(vmem_limit_bytes=VMEM_BYTES),
-        cost_estimate=pl.CostEstimate(
-            flops=heads * surv * surv * 600, bytes_accessed=heads * surv * surv * 4,
-            transcendentals=heads * surv * surv
+        scratch_shapes=[
+            pltpu.VMEM((shards, room, model), BF),
+            pltpu.VMEM((surv, surv), F32),
+            pltpu.VMEM((surv, width), BF),
+            pltpu.VMEM((shards * room, width), BF),
+            pltpu.VMEM((shards * room, width), BF),
+            pltpu.VMEM((width, model), F32),
+            pltpu.SemaphoreType.DMA((3, shards)),
+            pltpu.SemaphoreType.DMA((shards,)),
+            pltpu.SemaphoreType.DMA,
+        ],
+        compiler_params=pltpu.CompilerParams(
+            vmem_limit_bytes=VMEM_BYTES, collective_id=1, has_side_effects=True
         ),
-        name="forward_heads",
-    )(q, k, v)
+        name="gather_forward",
+    )(compact, grads, w, pack, q, k, v)
 
 
 def backward_kernel(
@@ -226,19 +397,11 @@
     place = (row[:, None] == local[None, :]).astype(BF)
     compact = (local[:, None] == row[None, :]).astype(BF)
 
-    sent = dot_nn(compact, grads[0]).astype(BF)
-    gathered = lax.all_gather(sent, "ctx", axis=0, tiled=True)
-
     q, k, v = queries[0], keys[0], values[0]
-    probs, outputs = forward_heads(q, k, v)
-    outputs = dot_nn(pack, outputs).astype(BF)
-
-    partial = dot_tn(outputs, gathered).astype(BF)
+    probs, head_grads, partial = gather_forward(
+        compact, grads[0], projector, pack, q, k, v, shards
+    )
     projector_derivative = lax.psum(partial, "dp").astype(F32)
-
-    gathered, _ = lax.optimization_barrier((gathered, partial))
-    slot_grads = dot_nt(gathered, projector).astype(BF)
-    head_grads = dot_tn(pack, slot_grads).astype(BF)
     received = backward_heads(q, k, v, head_grads, probs, pack, shards)
     every_place = place_rows(place, received)
     return (every_place[None], projector_derivative)

time: 194 us -> 180 us (0.928)
  Pallas kernels: 101 us -> 156 us
  waiting for transfers between devices: 50.7 us -> 0.02 us
  matrix products: 19.4 us -> 0 us
    all_gather x1 -> x0, waiting for transfers between devices: 50.6 us -> none  [body(): gathered = lax.all_gather(sent, 'ctx', axis=0, tiled=True)]
    pallas_call x1, Pallas kernels: 8.31 us -> 57.1 us  [gather_forward(): pl.pallas_call(gather_kernel, in_specs=[whole] * 7, out_specs=[pl.BlockSp...]
    dot_general x3 -> x0, matrix products: 19.4 us -> none  [the longest x2 16.9 us: dot_tn(): lax.dot_general(a, b, (((0,), (0,)), ((), ())), preferred_element_type=F32)]
    pallas_call x1, Pallas kernels: 86.5 us -> 93.3 us  [backward_heads(): pl.pallas_call(backward_kernel, grid=(heads,), in_specs=[rows] * 4 + [pl....]
  transfers between devices with their start and end apart: 2 -> 1, of which waited for: 1 -> 0; matrix products, arithmetic and copies ran while one was open for 5% -> 0% of each run, Pallas kernels for 52% -> 55%
where the time goes in v3:
time: 180 us
  Pallas kernels  156 us (87%)
  between operations  14.1 us (8%)
  other arithmetic  8.92 us (5%)
    pallas_call x1, Pallas kernels, backward_heads(): pl.pallas_call(backward_kernel, grid=(heads,), in_specs=[rows] * 4 + [pl....  93.3 us
    pallas_call x1, Pallas kernels, gather_forward(): pl.pallas_call(gather_kernel, in_specs=[whole] * 7, out_specs=[pl.BlockSp...  57.1 us
    pallas_call x1, Pallas kernels, place_rows(): pl.pallas_call(place_kernel, grid=(parts,), in_specs=[pl.BlockSpec(place....  5.74 us
    convert_element_type x1, other arithmetic, body(): projector_derivative = lax.psum(partial, 'dp').astype(F32)  4.78 us
  transfers between devices with their start and end apart: 1, of which 0 were waited for; matrix products, arithmetic and copies ran while one was open for 0% of the time, Pallas kernels for 55%

profile of v3, /device:TPU:11, one launch (start us, length us, event | category | flops | bytes accessed | tf_op | source)
XLA Modules:
  0.0 179.6 jit_solution(3632881198226982251)
XLA Ops:
  7.2 0.0 all-reduce.2.cloned.1.call-start
  7.2 0.7 fusion.3
  7.9 0.2 convert_reduce_fusion
  8.1 0.1 fusion.4
  8.2 0.1 iota_add_fusion
  8.3 0.1 add.44
  8.4 0.1 lt.37
  8.4 0.1 lt.38
  8.5 1.6 fusion.pack_ref
  10.1 0.1 dynamic_slice.3
  10.2 0.2 select_reduce_fusion
  10.4 0.7 fusion.2.compact_ref
  11.1 57.1 %gather_forward.1 = (f32[4,768,768]{2,1,0:T(8,128)}, bf16[768,512]{1,0:T(8,128)(2,1)}, bf16[512,2560]{1,0:T(8,128)(2,1)}) custom-call(bf16[144,192]{1,0:T(8,128)(2,1)} %fusion.2.compact_ref, bf16[192,2560]{1,0:T(8,128)(2,1)} %bitcast.6, bf16[512,2560]{1,0:T(8,128)(2,1)} %w_ref.1, bf16[1152,768]{1,0:T(8,128)(2,1)} %fusion.pack_ref, bf16[768,512]{1,0:T(8,128)(2,1)} %bitcast.7, ...), custom_call_target="tpu_custom_call" | custom-call | tf_op jit(solution)/shard_map/gather_forward/pallas_call | solution.py:214
  68.2 0.0 all-reduce.2.cloned.1.call-update
  68.3 0.7 fusion.1.place_ref
  68.9 93.3 %backward_heads.1.in_ref = bf16[8,4,3,144,128]{4,3,2,1,0:T(8,128)(2,1)} custom-call(bf16[768,512]{1,0:T(8,128)(2,1)} %bitcast.8, bf16[768,512]{1,0:T(8,128)(2,1)} %bitcast.10, bf16[768,512]{1,0:T(8,128)(2,1)} %bitcast.12, bf16[768,512]{1,0:T(8,128)(2,1)} %get-tuple-element.5.g_ref, f32[4,768,768]{2,1,0:T(8,128)} %get-tuple-element.6.probs_ref, ...), custom_call_target="tpu_custom_call" | custom-call | flops 47185920000 | bytes 9437184 | tf_op jit(solution)/shard_map/backward_heads/pallas_call | solution.py:322
  162.2 5.7 %place_rows.1 = bf16[192,12288]{1,0:T(8,128)(2,1)} custom-call(bf16[192,144]{1,0:T(8,128)(2,1)} %fusion.1.place_ref, bf16[8,4,3,144,128]{4,3,2,1,0:T(8,128)(2,1)} %backward_heads.1.in_ref), custom_call_target="tpu_custom_call" | custom-call | tf_op jit(solution)/shard_map/place_rows/pallas_call | solution.py:364
  167.9 0.0 all-reduce.2.cloned.1.call-done
  167.9 4.8 %convert_element_type.19 = f32[512,2560]{1,0:T(8,128)} convert(bf16[512,2560]{1,0:T(8,128)(2,1)} %all-reduce.2.cloned.1.call-done) | non-fusion elementwise | flops 1310720 | bytes 7864320 | tf_op jit(solution)/shard_map/convert_element_type | solution.py:404
  (3 shorter events, 0.0 us)
Async XLA Ops:
  7.2 160.8 %all-reduce.2.cloned.1.call-start = ((), (), s32[]{:S(2)}) async-start(), calls=%async_computation | async-start | bytes 5242880 | tf_op jit(solution)/shard_map/psum | solution.py:404
Sparse Core Ops, SparseCore 0:
  68.4 86.8 all-reduce.1

commit v4 on v3

--- a/solution.py
+++ b/solution.py
@@ -239,12 +239,45 @@
 
 
 def backward_kernel(
-    q_ref, k_ref, v_ref, g_ref, probs_ref, pack_ref, recv_ref, gk, gv, joined, outbox, send_sem, recv_sem, own_sem
+    q_ref, k_ref, v_ref, g_ref, probs_ref, pack_ref, partial_ref,
+    recv_ref, sum_ref,
+    gk, gv, joined, outbox, inbox, summed,
+    send_sem, recv_sem, own_sem, sum_send, sum_recv, sum_own,
 ):
     head = pl.program_id(0)
     heads, shards, _, room, _ = outbox.shape
     me, group = lax.axis_index("ctx"), lax.axis_index("dp")
     peers = [lax.rem(me + offset, shards) for offset in range(1, shards)]
+    groups, piece, _ = inbox.shape
+    others = [lax.rem(group + offset, groups) for offset in range(1, groups)]
+
+    def piece_rows(owner):
+        return pl.ds(pl.multiple_of(owner * piece, 16), piece)
+
+    def scatter(owner, source):
+        return pltpu.make_async_remote_copy(
+            src_ref=partial_ref.at[piece_rows(owner)],
+            dst_ref=inbox.at[source],
+            send_sem=sum_send.at[0, owner],
+            recv_sem=sum_recv.at[0, source],
+            device_id=(owner, me),
+            device_id_type=pl.DeviceIdType.MESH,
+        )
+
+    def spread(target, owner):
+        return pltpu.make_async_remote_copy(
+            src_ref=summed,
+            dst_ref=sum_ref.at[piece_rows(owner)],
+            send_sem=sum_send.at[1, target],
+            recv_sem=sum_recv.at[1, owner],
+            device_id=(target, me),
+            device_id_type=pl.DeviceIdType.MESH,
+        )
+
+    scatter_own = pltpu.make_async_copy(
+        partial_ref.at[piece_rows(group)], inbox.at[group], sum_own.at[0]
+    )
+    spread_own = pltpu.make_async_copy(summed, sum_ref.at[piece_rows(group)], sum_own.at[1])
 
     @pl.when(head == 0)
     def _():
@@ -253,7 +286,14 @@
             pl.semaphore_signal(
                 barrier, inc=1, device_id=(group, peer), device_id_type=pl.DeviceIdType.MESH
             )
-        pl.semaphore_wait(barrier, shards - 1)
+        for target in others:
+            pl.semaphore_signal(
+                barrier, inc=1, device_id=(target, me), device_id_type=pl.DeviceIdType.MESH
+            )
+        pl.semaphore_wait(barrier, shards - 1 + groups - 1)
+        for owner in others:
+            scatter(owner, group).start()
+        scatter_own.start()
 
     def outgoing(h, peer):
         return pltpu.make_async_remote_copy(
@@ -307,14 +347,29 @@
 
     @pl.when(head == heads - 1)
     def _():
+        scatter_own.wait()
+        for source in others:
+            scatter(source, source).wait_recv()
+        run = inbox[0].astype(F32)
+        for source in range(1, groups):
+            run = run + inbox[source].astype(F32)
+        summed[...] = run.astype(BF)
+        for target in others:
+            spread(target, group).start()
+        spread_own.start()
         for h in range(heads):
             own(h).wait()
             for peer in peers:
                 outgoing(h, peer).wait_send()
                 incoming(h, peer).wait_recv()
-
-
-def backward_heads(q, k, v, g, probs, pack, shards):
+        for target in others:
+            scatter(target, group).wait_send()
+            spread(target, group).wait_send()
+            spread(target, target).wait_recv()
+        spread_own.wait()
+
+
+def backward_heads(q, k, v, g, probs, pack, partial, shards, groups):
     surv, width = q.shape
     heads = width // HEAD_DIM
     room = pack.shape[0] // shards
@@ -326,17 +381,26 @@
         + [
             pl.BlockSpec((1, surv, surv), lambda h: (h, 0, 0)),
             pl.BlockSpec(pack.shape, lambda h: (0, 0)),
-        ],
-        out_specs=pl.BlockSpec(memory_space=pl.ANY),
-        out_shape=jax.ShapeDtypeStruct((shards, heads, 3, room, HEAD_DIM), BF),
+            pl.BlockSpec(memory_space=pl.ANY),
+        ],
+        out_specs=[pl.BlockSpec(memory_space=pl.ANY)] * 2,
+        out_shape=[
+            jax.ShapeDtypeStruct((shards, heads, 3, room, HEAD_DIM), BF),
+            jax.ShapeDtypeStruct(partial.shape, BF),
+        ],
         scratch_shapes=[
             pltpu.VMEM((surv, HEAD_DIM), F32),
             pltpu.VMEM((surv, HEAD_DIM), F32),
             pltpu.VMEM((surv, 3 * HEAD_DIM), BF),
             pltpu.VMEM((heads, shards, 3, room, HEAD_DIM), BF),
+            pltpu.VMEM((groups, width // groups, partial.shape[1]), BF),
+            pltpu.VMEM((width // groups, partial.shape[1]), BF),
             pltpu.SemaphoreType.DMA((heads, shards)),
             pltpu.SemaphoreType.DMA((heads, shards)),
             pltpu.SemaphoreType.DMA((heads,)),
+            pltpu.SemaphoreType.DMA((2, groups)),
+            pltpu.SemaphoreType.DMA((2, groups)),
+            pltpu.SemaphoreType.DMA((2,)),
         ],
         compiler_params=pltpu.CompilerParams(
             vmem_limit_bytes=VMEM_BYTES, collective_id=0, has_side_effects=True
@@ -346,33 +410,43 @@
             transcendentals=0
         ),
         name="backward_heads",
-    )(q, k, v, g, probs, pack)
-
-
-def place_kernel(place_ref, in_ref, out_ref):
+    )(q, k, v, g, probs, pack, partial)
+
+
+def place_kernel(place_ref, in_ref, sum_ref, out_ref, wide_ref):
     shards, heads, _, _, dim = in_ref.shape
     width = heads * dim
+
+    @pl.when(pl.program_id(0) == 0)
+    def _():
+        wide_ref[...] = sum_ref[...].astype(F32)
+
     for shard in range(shards):
         held = jnp.concatenate([in_ref[shard, h, 0] for h in range(heads)], axis=1)
         out_ref[:, shard * width : (shard + 1) * width] = dot_nn(place_ref[...], held).astype(BF)
 
 
-def place_rows(place, received):
+def place_rows(place, received, total):
     shards, heads, parts, room, dim = received.shape
     rows = place.shape[0]
     width = shards * heads * dim
+    wide = pl.BlockSpec((total.shape[0] // 2, total.shape[1]), lambda p, s: (jnp.minimum(2 * p + s, 1), 0))
     return pl.pallas_call(
         place_kernel,
-        grid=(parts,),
+        grid=(parts, 2),
         in_specs=[
-            pl.BlockSpec(place.shape, lambda p: (0, 0)),
-            pl.BlockSpec((shards, heads, 1, room, dim), lambda p: (0, 0, p, 0, 0)),
-        ],
-        out_specs=pl.BlockSpec((rows, width), lambda p: (0, p)),
-        out_shape=jax.ShapeDtypeStruct((rows, parts * width), BF),
+            pl.BlockSpec(place.shape, lambda p, s: (0, 0)),
+            pl.BlockSpec((shards // 2, heads, 1, room, dim), lambda p, s: (s, 0, p, 0, 0)),
+            wide,
+        ],
+        out_specs=[pl.BlockSpec((rows, width // 2), lambda p, s: (0, 2 * p + s)), wide],
+        out_shape=[
+            jax.ShapeDtypeStruct((rows, parts * width), BF),
+            jax.ShapeDtypeStruct(total.shape, F32),
+        ],
         compiler_params=pltpu.CompilerParams(vmem_limit_bytes=VMEM_BYTES),
         name="place_rows",
-    )(place, received)
+    )(place, received, total)
 
 
 def body(places, grads, projector, queries, keys, values):
@@ -401,9 +475,10 @@
     probs, head_grads, partial = gather_forward(
         compact, grads[0], projector, pack, q, k, v, shards
     )
-    projector_derivative = lax.psum(partial, "dp").astype(F32)
-    received = backward_heads(q, k, v, head_grads, probs, pack, shards)
-    every_place = place_rows(place, received)
+    received, total = backward_heads(
+        q, k, v, head_grads, probs, pack, partial, shards, lax.axis_size("dp")
+    )
+    every_place, projector_derivative = place_rows(place, received, total)
     return (every_place[None], projector_derivative)
 
 

time: 180 us -> 164 us (0.911)
  between operations: 14.1 us -> 0.69 us
  other arithmetic: 8.92 us -> 4.12 us
  Pallas kernels: 156 us -> 159 us
    convert_element_type x1 -> x0, other arithmetic: 4.78 us -> none  [body(): projector_derivative = lax.psum(partial, 'dp').astype(F32)]
    pallas_call x1, Pallas kernels: 5.74 us -> 8.29 us  [place_rows(): pl.pallas_call(place_kernel, grid=(parts, 2), in_specs=[pl.BlockSpec(plac...]
  transfers between devices with their start and end apart: 1 -> 0, of which waited for: 0 -> 0; matrix products, arithmetic and copies ran while one was open for 0% -> 0% of each run, Pallas kernels for 55% -> 0%
where the time goes in v4:
time: 164 us
  Pallas kernels  159 us (97%)
  other arithmetic  4.12 us (3%)
    pallas_call x1, Pallas kernels, backward_heads(): pl.pallas_call(backward_kernel, grid=(heads,), in_specs=[rows] * 4 + [pl....  93.5 us
    pallas_call x1, Pallas kernels, gather_forward(): pl.pallas_call(gather_kernel, in_specs=[whole] * 7, out_specs=[pl.BlockSp...  57.2 us
    pallas_call x1, Pallas kernels, place_rows(): pl.pallas_call(place_kernel, grid=(parts, 2), in_specs=[pl.BlockSpec(plac...  8.29 us

profile of v4, /device:TPU:11, one launch (start us, length us, event | category | flops | bytes accessed | tf_op | source)
XLA Modules:
  0.0 164.2 jit_solution(5782117882492258497)
XLA Ops:
  0.6 0.7 fusion.3
  1.4 0.2 convert_reduce_fusion
  1.5 0.1 fusion.4
  1.6 0.1 iota_add_fusion
  1.7 0.1 add.42
  1.8 0.1 lt.37
  1.8 0.1 lt.38
  2.0 0.1 dynamic_slice.3
  2.0 0.2 select_reduce_fusion
  2.3 0.7 fusion.2.compact_ref
  3.0 1.6 fusion.pack_ref
  4.5 57.2 %gather_forward.1 = (f32[4,768,768]{2,1,0:T(8,128)}, bf16[768,512]{1,0:T(8,128)(2,1)}, bf16[512,2560]{1,0:T(8,128)(2,1)}) custom-call(bf16[144,192]{1,0:T(8,128)(2,1)} %fusion.2.compact_ref, bf16[192,2560]{1,0:T(8,128)(2,1)} %bitcast.5, bf16[512,2560]{1,0:T(8,128)(2,1)} %w_ref.1, bf16[1152,768]{1,0:T(8,128)(2,1)} %fusion.pack_ref, bf16[768,512]{1,0:T(8,128)(2,1)} %bitcast.6, ...), custom_call_target="tpu_custom_call" | custom-call | tf_op jit(solution)/shard_map/gather_forward/pallas_call | solution.py:214
  61.8 93.5 %backward_heads.1 = (bf16[8,4,3,144,128]{4,3,2,1,0:T(8,128)(2,1)}, bf16[512,2560]{1,0:T(8,128)(2,1)}) custom-call(bf16[768,512]{1,0:T(8,128)(2,1)} %bitcast.7, bf16[768,512]{1,0:T(8,128)(2,1)} %bitcast.9, bf16[768,512]{1,0:T(8,128)(2,1)} %bitcast.11, bf16[768,512]{1,0:T(8,128)(2,1)} %get-tuple-element.9.g_ref, f32[4,768,768]{2,1,0:T(8,128)} %get-tuple-element.10.probs_ref, ...), custom_call_target="tpu_custom_call" | custom-call | flops 47185920000 | bytes 9437184 | tf_op jit(solution)/shard_map/backward_heads/pallas_call | solution.py:377
  155.3 0.6 fusion.1.place_ref
  155.9 8.3 %place_rows.1 = (bf16[192,12288]{1,0:T(8,128)(2,1)}, f32[512,2560]{1,0:T(8,128)}) custom-call(bf16[192,144]{1,0:T(8,128)(2,1)} %fusion.1.place_ref, bf16[8,4,3,144,128]{4,3,2,1,0:T(8,128)(2,1)} %get-tuple-element.12.in_ref, bf16[512,2560]{1,0:T(8,128)(2,1)} %get-tuple-element.13.sum_ref), custom_call_target="tpu_custom_call" | custom-call | tf_op jit(solution)/shard_map/place_rows/pallas_call | solution.py:434
  (3 shorter events, 0.0 us)

commit v5 on v4

--- a/solution.py
+++ b/solution.py
@@ -32,9 +32,10 @@
 
 
 def gather_kernel(
-    compact_ref, grads_ref, w_ref, pack_ref, q_ref, k_ref, v_ref,
+    compact_ref, grads_ref, w_hbm, pack_hbm, q_hbm, k_hbm, v_hbm,
     probs_ref, head_grads_ref, partial_ref,
-    blocks, stage, outputs, slot_outputs, slot_grads, total, send_sem, recv_sem, stage_sem,
+    w_ref, pack_ref, q_ref, k_ref, v_ref,
+    blocks, stage, outputs, slot_outputs, picked_grads, total, send_sem, recv_sem, stage_sem, load_sem,
 ):
     shards, room, _ = blocks.shape
     surv, width = q_ref.shape
@@ -45,7 +46,14 @@
     other = chip * 2 + (1 - core)
     after, before = lax.rem(me + 2, shards), lax.rem(me + shards - 2, shards)
 
-    blocks[me] = dot_nn(compact_ref[...], grads_ref[...]).astype(BF)
+    sources = (q_hbm, k_hbm, v_hbm, pack_hbm, w_hbm)
+    targets = (q_ref, k_ref, v_ref, pack_ref, w_ref)
+    loads = [
+        pltpu.make_async_copy(source, target, load_sem.at[i])
+        for i, (source, target) in enumerate(zip(sources, targets))
+    ]
+    for load in loads:
+        load.start()
 
     barrier = pltpu.get_barrier_semaphore()
     for offset in range(1, shards):
@@ -53,6 +61,7 @@
             barrier, inc=1, device_id=(group, lax.rem(me + offset, shards)),
             device_id_type=pl.DeviceIdType.MESH,
         )
+    blocks[me] = dot_nn(compact_ref[...], grads_ref[...]).astype(BF)
     pl.semaphore_wait(barrier, shards - 1)
 
     def hop(slot, way, target):
@@ -83,6 +92,8 @@
         down(me).start()
 
     across(me).start()
+    for load in loads:
+        load.wait()
 
     scale = 1.0 / math.sqrt(HEAD_DIM)
 
@@ -115,10 +126,12 @@
 
     def work(slot):
         rows = pl.ds(pl.multiple_of(slot * room, 16), room)
-        slot_grads[rows, :] = dot_nt(blocks[slot], w_ref[...]).astype(BF)
+        slot_grads = dot_nt(blocks[slot], w_ref[...]).astype(BF)
+        picked_grads[...] += dot_tn(pack_ref[rows, :], slot_grads)
         total[...] += dot_tn(slot_outputs[rows, :], blocks[slot])
 
     total[...] = jnp.zeros_like(total)
+    picked_grads[...] = jnp.zeros_like(picked_grads)
     work(me)
     across(other).wait_recv()
     work(other)
@@ -168,7 +181,7 @@
 
     lax.fori_loop(1, chips, step, 0)
 
-    head_grads_ref[...] = dot_tn(pack_ref[...], slot_grads[...]).astype(BF)
+    head_grads_ref[...] = picked_grads[...].astype(BF)
     partial_ref[...] = total[...].astype(BF)
 
     across(me).wait_send()
@@ -213,7 +226,7 @@
     whole = pl.BlockSpec(memory_space=pltpu.VMEM)
     return pl.pallas_call(
         gather_kernel,
-        in_specs=[whole] * 7,
+        in_specs=[whole] * 2 + [pl.BlockSpec(memory_space=pl.ANY)] * 5,
         out_specs=[pl.BlockSpec(memory_space=pl.ANY), whole, whole],
         out_shape=[
             jax.ShapeDtypeStruct((heads, surv, surv), F32),
@@ -221,15 +234,21 @@
             jax.ShapeDtypeStruct((width, model), BF),
         ],
         scratch_shapes=[
+            pltpu.VMEM(w.shape, BF),
+            pltpu.VMEM(pack.shape, BF),
+            pltpu.VMEM(q.shape, BF),
+            pltpu.VMEM(q.shape, BF),
+            pltpu.VMEM(q.shape, BF),
             pltpu.VMEM((shards, room, model), BF),
             pltpu.VMEM((surv, surv), F32),
             pltpu.VMEM((surv, width), BF),
             pltpu.VMEM((shards * room, width), BF),
-            pltpu.VMEM((shards * room, width), BF),
+            pltpu.VMEM((surv, width), F32),
             pltpu.VMEM((width, model), F32),
             pltpu.SemaphoreType.DMA((3, shards)),
             pltpu.SemaphoreType.DMA((shards,)),
             pltpu.SemaphoreType.DMA,
+            pltpu.SemaphoreType.DMA((5,)),
         ],
         compiler_params=pltpu.CompilerParams(
             vmem_limit_bytes=VMEM_BYTES, collective_id=1, has_side_effects=True

time: 164 us -> 162 us (0.988)
  Pallas kernels: 159 us -> 156 us
    pallas_call x1, Pallas kernels: 57.2 us -> 54.8 us  [gather_forward(): pl.pallas_call(gather_kernel, in_specs=[whole] * 2 + [pl.BlockSpec(memory...]
where the time goes in v5:
time: 162 us; the launch traced here: 161 us
  Pallas kernels  156 us (96%)
  other arithmetic  4.12 us (3%)
    pallas_call x1, Pallas kernels, backward_heads(): pl.pallas_call(backward_kernel, grid=(heads,), in_specs=[rows] * 4 + [pl....  93 us
    pallas_call x1, Pallas kernels, gather_forward(): pl.pallas_call(gather_kernel, in_specs=[whole] * 2 + [pl.BlockSpec(memory...  54.8 us
    pallas_call x1, Pallas kernels, place_rows(): pl.pallas_call(place_kernel, grid=(parts, 2), in_specs=[pl.BlockSpec(plac...  8.29 us

profile of v5, /device:TPU:11, one launch (start us, length us, event | category | flops | bytes accessed | tf_op | source)
XLA Modules:
  0.0 161.3 jit_solution(4852660011366575006)
XLA Ops:
  0.6 0.7 fusion.3
  1.4 0.2 convert_reduce_fusion
  1.5 0.1 fusion.4
  1.6 0.1 iota_add_fusion
  1.7 0.1 add.42
  1.8 0.1 lt.37
  1.8 0.1 lt.38
  2.0 0.1 dynamic_slice.3
  2.0 0.2 select_reduce_fusion
  2.3 0.7 fusion.2.compact_ref
  3.0 1.6 fusion.pack_hbm.pack_ref
  4.5 54.8 %gather_forward.1 = (f32[4,768,768]{2,1,0:T(8,128)}, bf16[768,512]{1,0:T(8,128)(2,1)}, bf16[512,2560]{1,0:T(8,128)(2,1)}) custom-call(bf16[144,192]{1,0:T(8,128)(2,1)} %fusion.2.compact_ref, bf16[192,2560]{1,0:T(8,128)(2,1)} %bitcast.5, bf16[512,2560]{1,0:T(8,128)(2,1)} %w_hbm.1, bf16[1152,768]{1,0:T(8,128)(2,1)} %fusion.pack_hbm.pack_ref, ...), custom_call_target="tpu_custom_call" | custom-call | tf_op jit(solution)/shard_map/gather_forward/pallas_call | solution.py:227
  59.4 93.0 %backward_heads.1 = (bf16[8,4,3,144,128]{4,3,2,1,0:T(8,128)(2,1)}, bf16[512,2560]{1,0:T(8,128)(2,1)}) custom-call(bf16[768,512]{1,0:T(8,128)(2,1)} %bitcast.7, bf16[768,512]{1,0:T(8,128)(2,1)} %bitcast.9, bf16[768,512]{1,0:T(8,128)(2,1)} %bitcast.11, bf16[768,512]{1,0:T(8,128)(2,1)} %get-tuple-element.9.g_ref, f32[4,768,768]{2,1,0:T(8,128)} %get-tuple-element.10.probs_ref, ...), custom_call_target="tpu_custom_call" | custom-call | flops 47185920000 | bytes 9437184 | tf_op jit(solution)/shard_map/backward_heads/pallas_call | solution.py:396
  152.3 0.6 fusion.1.place_ref
  153.0 8.3 %place_rows.1 = (bf16[192,12288]{1,0:T(8,128)(2,1)}, f32[512,2560]{1,0:T(8,128)}) custom-call(bf16[192,144]{1,0:T(8,128)(2,1)} %fusion.1.place_ref, bf16[8,4,3,144,128]{4,3,2,1,0:T(8,128)(2,1)} %get-tuple-element.12.in_ref, bf16[512,2560]{1,0:T(8,128)(2,1)} %get-tuple-element.13.sum_ref), custom_call_target="tpu_custom_call" | custom-call | tf_op jit(solution)/shard_map/place_rows/pallas_call | solution.py:453
  (3 shorter events, 0.0 us)
